TPU v7x, 128 devices: a whole 4x4x4 slice. The times are simulated.
128 devices in a mesh: seq: 16 (over z_hi, y, core), batch: 8 (over x, z_lo).
Axes of the slice: x: 4, y: 4, z: 4 (z_hi: 2, z_lo: 2; z = z_hi * 2 + z_lo), core: 2. Of those that a mesh axis runs over, the one named last changes fastest.
Arguments:
- tokens: bfloat16 [16, 1024, 1088], P('batch', 'seq'), may hold values from -6 to 6
- segments: int32 [16, 1024], P('batch', 'seq'), may hold values from 0 to 256, as said below
- adapter_pick: int32 [16], P('batch'), may hold values from 0 to 7
- norm_gain: float32 [2, 2, 1088], replicated, may hold values from 0.1 to 1.9
- w_qkv: bfloat16 [2, 3551232], P(None, ('seq', 'batch')), may hold values from -0.1875 to 0.1875
- w_out: bfloat16 [2, 1183744], P(None, ('seq', 'batch')), may hold values from -0.75 to 0.75
- w_up: bfloat16 [2, 4734976], P(None, ('seq', 'batch')), may hold values from -0.1875 to 0.1875
- w_down: bfloat16 [2, 4734976], P(None, ('seq', 'batch')), may hold values from -0.09375 to 0.09375
- a_qkv: bfloat16 [2, 1088, 128], replicated, may hold values from -0.1875 to 0.1875
- b_qkv: bfloat16 [2, 128, 3264], replicated, may hold values from -0.75 to 0.75
- a_out: bfloat16 [2, 1088, 128], replicated, may hold values from -0.1875 to 0.1875
- b_out: bfloat16 [2, 128, 1088], replicated, may hold values from -0.75 to 0.75
- a_up: bfloat16 [2, 1088, 128], replicated, may hold values from -0.1875 to 0.1875
- b_up: bfloat16 [2, 128, 4352], replicated, may hold values from -0.75 to 0.75
- a_down: bfloat16 [2, 4352, 128], replicated, may hold values from -0.09375 to 0.09375
- b_down: bfloat16 [2, 128, 1088], replicated, may hold values from -0.75 to 0.75
- grad_out: bfloat16 [16, 1024, 1088], P('batch', 'seq'), may hold values from -6 to 6
Outputs:
- out: bfloat16 [16, 1024, 1088], P('batch', 'seq')
- grad_tokens: float32 [16, 1024, 1088], P('batch', 'seq')
- grad_a_qkv: float32 [2, 1088, 128], replicated
- grad_b_qkv: float32 [2, 128, 3264], replicated
- grad_a_out: float32 [2, 1088, 128], replicated
- grad_b_out: float32 [2, 128, 1088], replicated
- grad_a_up: float32 [2, 1088, 128], replicated
- grad_b_up: float32 [2, 128, 4352], replicated
- grad_a_down: float32 [2, 4352, 128], replicated
- grad_b_down: float32 [2, 128, 1088], replicated
Inputs may be any that keep to these rules, and one draw needn't show every extreme that they name: `segments`: along each sequence the numbers start at 0 and rise by 0 or 1 from one position to the next; equal numbers mark one document. In one sequence of each group of 2 that share an index of batch, one document begins within the first 64 positions and ends within the last 64.
All inputs are finite; a program needn't handle non-finite values.
Results may differ from a plain program's by a relative error of at most 0.024.
Values may be sent and summed in bfloat16 or wider, within the bound.
No kernel may reach another device: no remote copies, remote signals or barrier semaphores. Data moves between devices by JAX's collectives and lax.ppermute only.
A program may use at most 320 MiB of HBM per device.

v0:
```python
from functools import partial
import math

import jax
import jax.numpy as jnp
from jax import lax
from jax.sharding import PartitionSpec as P

D = 1088
HEAD_DIM = 64
FF = 4352
ADAPTERS = 8
RANK = 16


def prefix(x, axis, combine, identity):
    count, position = (lax.axis_size(axis), lax.axis_index(axis))
    everything = jax.tree.map(lambda part: lax.all_gather(part, axis), x)
    start = jax.tree.map(
        lambda part, zero: jnp.broadcast_to(jnp.asarray(zero, part.dtype), part.shape), x, identity
    )

    def turn(k, before):
        reached = k < position
        new = combine(before, jax.tree.map(lambda part: part[k], everything))
        return jax.tree.map(lambda a, b: jnp.where(reached, a, b), new, before)

    return lax.fori_loop(0, count, turn, start)


def layer_norm(values, gain_row):
    row_mean = jnp.mean(values, axis=-1, keepdims=True)
    centred = values - row_mean
    spread = jnp.mean(centred * centred, axis=-1, keepdims=True)
    return centred * lax.rsqrt(spread + 1e-05) * gain_row


def dot_plain(left_side, right_side):
    return jnp.dot(left_side, right_side, preferred_element_type=jnp.float32)


def dot_right_t(left_side, right_side):
    return lax.dot_general(
        left_side, right_side, (((1,), (1,)), ((), ())), preferred_element_type=jnp.float32
    )


def dot_left_t(left_side, right_side):
    return lax.dot_general(
        left_side, right_side, (((0,), (0,)), ((), ())), preferred_element_type=jnp.float32
    )


def shape_layer(flat_parts):
    return (
        flat_parts[0].reshape(D, 3 * D),
        flat_parts[1].reshape(D, D),
        flat_parts[2].reshape(D, FF),
        flat_parts[3].reshape(FF, D),
    )


def project_fwd(normed, weight, adapter_in, adapter_out, mask_rows):
    lowrank = (dot_plain(normed, adapter_in) * mask_rows).astype(jnp.bfloat16)
    return (dot_plain(normed, weight) + dot_plain(lowrank, adapter_out), lowrank)


def project_back(grad_z, normed, lowrank, weight, adapter_in, adapter_out, mask_rows):
    grad_outer = dot_left_t(lowrank, grad_z)
    grad_low = (dot_right_t(grad_z, adapter_out) * mask_rows).astype(jnp.bfloat16)
    grad_inner = dot_left_t(normed, grad_low)
    grad_input = dot_right_t(grad_z, weight) + dot_right_t(grad_low, adapter_in)
    return (grad_input, grad_inner, grad_outer)


def split_heads(queries, pair_rows):
    micro_count, row_count, model_width = queries.shape
    head_count = model_width // HEAD_DIM
    query_heads = queries.reshape(micro_count, row_count, head_count, HEAD_DIM)
    key_heads = pair_rows[:, :, :model_width].reshape(micro_count, -1, head_count, HEAD_DIM)
    value_heads = pair_rows[:, :, model_width:].reshape(micro_count, -1, head_count, HEAD_DIM)
    return (query_heads, key_heads, value_heads)


def attend_fwd(queries, pair_rows, visible):
    micro_count, row_count, model_width = queries.shape
    score_scale = 1.0 / math.sqrt(HEAD_DIM)
    query_heads, key_heads, value_heads = split_heads(queries, pair_rows)
    scores = (
        jnp.einsum("mqhd,mkhd->mhqk", query_heads, key_heads, preferred_element_type=jnp.float32)
        * score_scale
    )
    scores = jnp.where(visible[:, None], scores, -1e30)
    top_score = jnp.max(scores, axis=-1, keepdims=True)
    row_lse = top_score + jnp.log(jnp.sum(jnp.exp(scores - top_score), axis=-1, keepdims=True))
    attn_probs = jnp.exp(scores - row_lse).astype(jnp.bfloat16)
    context = jnp.einsum(
        "mhqk,mkhd->mqhd", attn_probs, value_heads, preferred_element_type=jnp.float32
    )
    return (context.reshape(micro_count, row_count, model_width).astype(jnp.bfloat16), row_lse)


def attend_back(queries, pair_rows, visible, row_lse, grad_context):
    micro_count, row_count, model_width = queries.shape
    score_scale = 1.0 / math.sqrt(HEAD_DIM)
    query_heads, key_heads, value_heads = split_heads(queries, pair_rows)
    scores = (
        jnp.einsum("mqhd,mkhd->mhqk", query_heads, key_heads, preferred_element_type=jnp.float32)
        * score_scale
    )
    attn_probs = jnp.where(visible[:, None], jnp.exp(scores - row_lse), 0.0)
    grad_heads = grad_context.reshape(micro_count, row_count, -1, HEAD_DIM)
    grad_probs = jnp.einsum(
        "mqhd,mkhd->mhqk", grad_heads, value_heads, preferred_element_type=jnp.float32
    )
    row_delta = jnp.sum(attn_probs * grad_probs, axis=-1, keepdims=True)
    grad_scores = (attn_probs * (grad_probs - row_delta)).astype(jnp.bfloat16)
    grad_query = (
        jnp.einsum("mhqk,mkhd->mqhd", grad_scores, key_heads, preferred_element_type=jnp.float32)
        * score_scale
    )
    return (
        grad_query.reshape(micro_count, row_count, model_width),
        grad_scores,
        attn_probs.astype(jnp.bfloat16),
        query_heads,
        grad_heads,
        row_delta,
    )


def shards(
    tokens,
    segments,
    adapter_pick,
    norm_gain,
    w_qkv,
    w_out,
    w_up,
    w_down,
    a_qkv,
    b_qkv,
    a_out,
    b_out,
    a_up,
    b_up,
    a_down,
    b_down,
    grad_out,
):
    micro_count, shard_rows, model_width = tokens.shape
    layer_count = norm_gain.shape[0]
    all_rows = micro_count * shard_rows
    seq_count = lax.axis_size("seq")
    base_row = lax.axis_index("seq") * shard_rows
    score_scale = 1.0 / math.sqrt(HEAD_DIM)
    first_local = jnp.sum((segments[:, None, :] < segments[:, :, None]).astype(jnp.int32), axis=2)
    last_seg = segments[:, -1]

    def combine_runs(earlier, later):
        seg_early, start_early = earlier
        seg_late, start_late = later
        keep_early = (seg_late < 0) | (seg_late == seg_early)
        merged_seg = jnp.where(seg_late < 0, seg_early, seg_late)
        return (merged_seg, jnp.where(keep_early, start_early, start_late))

    prior_seg, prior_start = prefix(
        (last_seg, base_row + first_local[:, -1]),
        "seq",
        combine_runs,
        (jnp.full_like(last_seg, -1), jnp.zeros_like(last_seg)),
    )
    doc_start = jnp.where(
        (first_local == 0) & (segments == prior_seg[:, None]),
        prior_start[:, None],
        base_row + first_local,
    )
    query_pos = base_row + jnp.arange(shard_rows, dtype=jnp.int32)
    key_pos = jnp.arange(shard_rows * seq_count, dtype=jnp.int32)
    visible = (key_pos[None, None, :] <= query_pos[None, :, None]) & (
        key_pos[None, None, :] >= doc_start[:, :, None]
    )
    column_group = jnp.arange(ADAPTERS * RANK, dtype=jnp.int32) // RANK
    adapter_mask = (column_group[None, :] == adapter_pick[:, None]).astype(jnp.float32)
    mask_rows = jnp.repeat(adapter_mask, shard_rows, axis=0)
    hidden = tokens.reshape(all_rows, model_width).astype(jnp.float32)
    saved_layers = []
    for layer_idx in range(layer_count):
        gather_flat_parts = (
            lax.all_gather(w_qkv[layer_idx], ("seq", "batch"), axis=0, tiled=True),
            lax.all_gather(w_out[layer_idx], ("seq", "batch"), axis=0, tiled=True),
            lax.all_gather(w_up[layer_idx], ("seq", "batch"), axis=0, tiled=True),
            lax.all_gather(w_down[layer_idx], ("seq", "batch"), axis=0, tiled=True),
        )
        matrices = shape_layer(gather_flat_parts)
        normed = layer_norm(hidden, norm_gain[layer_idx, 0]).astype(jnp.bfloat16)
        projected, low_qkv = project_fwd(
            normed, matrices[0], a_qkv[layer_idx], b_qkv[layer_idx], mask_rows
        )
        projected = projected.astype(jnp.bfloat16)
        queries = projected[:, :model_width].reshape(micro_count, shard_rows, model_width)
        pair_local = projected[:, model_width:].reshape(micro_count, shard_rows, 2 * model_width)
        pair_rows = lax.all_gather(pair_local, "seq", axis=1, tiled=True)
        context, row_lse = attend_fwd(queries, pair_rows, visible)
        context = context.reshape(all_rows, model_width)
        branch, low_out = project_fwd(
            context, matrices[1], a_out[layer_idx], b_out[layer_idx], mask_rows
        )
        middle = hidden + branch
        normed_two = layer_norm(middle, norm_gain[layer_idx, 1]).astype(jnp.bfloat16)
        upward, low_up = project_fwd(
            normed_two, matrices[2], a_up[layer_idx], b_up[layer_idx], mask_rows
        )
        active = jax.nn.gelu(upward, approximate=False).astype(jnp.bfloat16)
        downward, low_down = project_fwd(
            active, matrices[3], a_down[layer_idx], b_down[layer_idx], mask_rows
        )
        saved_layers.append(
            (
                hidden,
                normed,
                low_qkv,
                queries,
                pair_local,
                pair_rows,
                row_lse,
                context,
                low_out,
                middle,
                normed_two,
                low_up,
                upward,
                active,
                low_down,
                matrices,
            )
        )
        hidden = middle + downward
    result = hidden.astype(jnp.bfloat16).reshape(micro_count, shard_rows, model_width)
    grad_hidden = grad_out.reshape(all_rows, model_width).astype(jnp.float32)
    grads_by_layer = [None] * layer_count
    for layer_idx in reversed(range(layer_count)):
        (
            hidden_in,
            normed,
            low_qkv,
            queries,
            pair_local,
            pair_rows,
            row_lse,
            context,
            low_out,
            middle,
            normed_two,
            low_up,
            upward,
            active,
            low_down,
            kept_matrices,
        ) = saved_layers[layer_idx]
        flat_parts = (
            lax.all_gather(w_qkv[layer_idx], ("seq", "batch"), axis=0, tiled=True),
            lax.all_gather(w_out[layer_idx], ("seq", "batch"), axis=0, tiled=True),
            lax.all_gather(w_up[layer_idx], ("seq", "batch"), axis=0, tiled=True),
            lax.all_gather(w_down[layer_idx], ("seq", "batch"), axis=0, tiled=True),
        )
        matrices = shape_layer(flat_parts)
        grad_act, inner_down, outer_down = project_back(
            grad_hidden.astype(jnp.bfloat16),
            active,
            low_down,
            matrices[3],
            a_down[layer_idx],
            b_down[layer_idx],
            mask_rows,
        )
        gelu_value, gelu_pull = jax.vjp(partial(jax.nn.gelu, approximate=False), upward)
        grad_up = gelu_pull(grad_act)[0].astype(jnp.bfloat16)
        grad_normed_two, inner_up, outer_up = project_back(
            grad_up, normed_two, low_up, matrices[2], a_up[layer_idx], b_up[layer_idx], mask_rows
        )
        norm_value, norm_pull = jax.vjp(
            partial(layer_norm, gain_row=norm_gain[layer_idx, 1]), middle
        )
        grad_middle = grad_hidden + norm_pull(grad_normed_two)[0]
        grad_context, inner_out, outer_out = project_back(
            grad_middle.astype(jnp.bfloat16),
            context,
            low_out,
            matrices[1],
            a_out[layer_idx],
            b_out[layer_idx],
            mask_rows,
        )
        grad_context = grad_context.astype(jnp.bfloat16).reshape(
            micro_count, shard_rows, model_width
        )
        grad_query, grad_scores, soft_weights, query_heads, grad_heads, row_delta = attend_back(
            queries, pair_rows, visible, row_lse, grad_context
        )
        row_count = shard_rows * lax.axis_size("seq")
        grad_keys = (
            jnp.einsum(
                "mhqk,mqhd->kmhd", grad_scores, query_heads, preferred_element_type=jnp.float32
            )
            * score_scale
        )
        grad_values = jnp.einsum(
            "mhqk,mqhd->kmhd", soft_weights, grad_heads, preferred_element_type=jnp.float32
        )
        pair_grads = lax.psum_scatter(
            jnp.concatenate(
                [
                    grad_keys.reshape(row_count, micro_count, model_width),
                    grad_values.reshape(row_count, micro_count, model_width),
                ],
                axis=2,
            ).astype(jnp.bfloat16),
            "seq",
            scatter_dimension=0,
            tiled=True,
        ).astype(jnp.float32)
        pair_block = jnp.transpose(pair_grads, (1, 0, 2))
        grad_projected = jnp.concatenate([grad_query, pair_block], axis=2)
        grad_projected = grad_projected.reshape(all_rows, 3 * model_width).astype(jnp.bfloat16)
        grad_normed, inner_qkv, outer_qkv = project_back(
            grad_projected,
            normed,
            low_qkv,
            matrices[0],
            a_qkv[layer_idx],
            b_qkv[layer_idx],
            mask_rows,
        )
        first_value, first_pull = jax.vjp(
            partial(layer_norm, gain_row=norm_gain[layer_idx, 0]), hidden_in
        )
        grad_hidden = grad_middle + first_pull(grad_normed)[0]
        grads_by_layer[layer_idx] = (
            inner_qkv,
            outer_qkv,
            inner_out,
            outer_out,
            inner_up,
            outer_up,
            inner_down,
            outer_down,
        )
    stacked = [
        jnp.stack([grads_by_layer[layer_idx][member] for layer_idx in range(layer_count)])
        for member in range(8)
    ]
    summed = lax.psum(
        (
            stacked[0],
            stacked[1],
            stacked[2],
            stacked[3],
            stacked[4],
            stacked[5],
            stacked[6],
            stacked[7],
        ),
        ("seq", "batch"),
    )
    grad_tokens = grad_hidden.reshape(micro_count, shard_rows, model_width)
    return (
        result,
        grad_tokens,
        summed[0],
        summed[1],
        summed[2],
        summed[3],
        summed[4],
        summed[5],
        summed[6],
        summed[7],
    )


def solution(mesh):
    in_specs = (
        P("batch", "seq", None),
        P("batch", "seq"),
        P("batch"),
        P(),
        P(None, ("seq", "batch")),
        P(None, ("seq", "batch")),
        P(None, ("seq", "batch")),
        P(None, ("seq", "batch")),
        P(),
        P(),
        P(),
        P(),
        P(),
        P(),
        P(),
        P(),
        P("batch", "seq", None),
    )
    out_specs = (
        P("batch", "seq", None),
        P("batch", "seq", None),
        P(),
        P(),
        P(),
        P(),
        P(),
        P(),
        P(),
        P(),
    )
    return jax.shard_map(shards, mesh=mesh, in_specs=in_specs, out_specs=out_specs, check_vma=False)
```

profile of v0, /device:TPU:1, one launch (start us, length us, event | category | flops | bytes accessed | tf_op | source)
XLA Modules:
  0.0 2545.5 jit_solution(6048105879832980334)
XLA Ops:
  27.9 220.4 %all-reduce.14.cloned.1.call-done = (bf16[3551232]{0:T(1024)(128)(2,1)}, bf16[1183744]{0:T(1024)(128)(2,1)}, bf16[3551232]{0:T(1024)(128)(2,1)}, bf16[1183744]{0:T(1024)(128)(2,1)}) async-done(((bf16[3551232]{0:T(1024)(128)(2,1)}, bf16[1183744]{0:T(1024)(128)(2,1)}, bf16[3551232]{0:T(1024)(128)(2,1)}, bf16[1183744]{0:T(1024)(128)(2,1)}), (bf16[3551232]{0:T(1024)(128)(2,1)}, bf16[1183744]{0:T(1024)(128)(2,1)}, ...) | async-done | bytes 18939920
  248.3 13.1 reshape.365
  272.8 10.3 all-reduce.6
  289.9 13.5 reshape.373
  303.3 277.2 %all-gather.21.cloned.1.call-done = bf16[1,4734976]{1,0:T(2,128)(2,1)} async-done(((bf16[1,36992]{1,0:T(2,128)(2,1)}), bf16[1,4734976]{1,0:T(2,128)(2,1)}) %all-gather.21.cloned.1.call-update) | async-done | bytes 9469968 | tf_op jit(solution)/shard_map/all_gather | solution.py:192
  580.6 201.5 %reduce.8 = bf16[4734976]{0:T(1024)(128)(2,1)} reduce(bf16[1,4734976]{1,0:T(2,128)(2,1)} %all-gather.21.cloned.1.call-done, bf16[]{:T(256)} %constant.181), dimensions={0}, to_apply=%all-gather.4.reduce_sub_computation | reduce | bytes 18939906 | tf_op jit(solution)/shard_map/all_gather | solution.py:192
  782.0 17.8 reshape.371
  799.8 114.9 %all-gather.23.cloned.1.call-done = bf16[1,4734976]{1,0:T(2,128)(2,1)} async-done(((bf16[1,36992]{1,0:T(2,128)(2,1)}), bf16[1,4734976]{1,0:T(2,128)(2,1)}) %all-gather.23.cloned.1.call-update) | async-done | bytes 9469968 | tf_op jit(solution)/shard_map/all_gather | solution.py:193
  914.7 201.6 %reduce.9 = bf16[4734976]{0:T(1024)(128)(2,1)} reduce(bf16[1,4734976]{1,0:T(2,128)(2,1)} %all-gather.23.cloned.1.call-done, bf16[]{:T(256)} %constant.181), dimensions={0}, to_apply=%all-gather.5.reduce_sub_computation | reduce | bytes 18939906 | tf_op jit(solution)/shard_map/all_gather | solution.py:193
  1116.4 17.1 reshape.372
  1133.4 10.1 fusion.197
  1205.3 119.3 %all-gather.25.cloned.1.call-done = bf16[1,4734976]{1,0:T(2,128)(2,1)} async-done(((bf16[1,36992]{1,0:T(2,128)(2,1)}), bf16[1,4734976]{1,0:T(2,128)(2,1)}) %all-gather.25.cloned.1.call-update) | async-done | bytes 9469968 | tf_op jit(solution)/shard_map/all_gather | solution.py:192
  1324.6 201.5 %reduce.14 = bf16[4734976]{0:T(1024)(128)(2,1)} reduce(bf16[1,4734976]{1,0:T(2,128)(2,1)} %all-gather.25.cloned.1.call-done, bf16[]{:T(256)} %constant.181), dimensions={0}, to_apply=%all-gather.8.reduce_sub_computation | reduce | bytes 18939906 | tf_op jit(solution)/shard_map/all_gather | solution.py:192
  1526.1 17.8 reshape.378
  1543.9 114.7 %all-gather.27.cloned.1.call-done = bf16[1,4734976]{1,0:T(2,128)(2,1)} async-done(((bf16[1,36992]{1,0:T(2,128)(2,1)}), bf16[1,4734976]{1,0:T(2,128)(2,1)}) %all-gather.27.cloned.1.call-update) | async-done | bytes 9469968 | tf_op jit(solution)/shard_map/all_gather | solution.py:193
  1658.6 201.6 %reduce.15 = bf16[4734976]{0:T(1024)(128)(2,1)} reduce(bf16[1,4734976]{1,0:T(2,128)(2,1)} %all-gather.27.cloned.1.call-done, bf16[]{:T(256)} %constant.181), dimensions={0}, to_apply=%all-gather.9.reduce_sub_computation | reduce | bytes 18939906 | tf_op jit(solution)/shard_map/all_gather | solution.py:193
  1860.2 17.0 reshape.379
  1887.3 9.9 fusion.196
  1959.1 11.6 multiply_reduce_fusion.1
  1994.7 9.3 pad_maximum_fusion
  2010.0 98.1 %reduce-scatter.3.cloned.1.call-done = bf16[64,2,2176]{2,0,1:T(8,128)(2,1)} async-done(((bf16[1024,2,2176]{2,0,1:T(8,128)(2,1)}), bf16[64,2,2176]{2,0,1:T(8,128)(2,1)}) %reduce-scatter.3.cloned.1.call-update) | async-done | bytes 557072 | tf_op jit(solution)/shard_map/reduce_scatter | solution.py:311
  2138.2 11.5 multiply_reduce_fusion
  2222.8 64.3 %reduce-scatter.5.cloned.1.call-done = bf16[64,2,2176]{2,0,1:T(8,128)(2,1)} async-done(((bf16[1024,2,2176]{2,0,1:T(8,128)(2,1)}), bf16[64,2,2176]{2,0,1:T(8,128)(2,1)}) %reduce-scatter.5.cloned.1.call-update) | async-done | bytes 557072 | tf_op jit(solution)/shard_map/reduce_scatter | solution.py:311
  2310.3 211.5 %all-reduce.12.cloned.1.call-done = (f32[2,1088,128]{2,1,0:T(8,128)}, f32[2,128,3264]{1,2,0:T(8,128)}, f32[2,1088,128]{2,1,0:T(8,128)}, f32[2,128,1088]{1,2,0:T(...) async-done(((f32[2,1088,128]{2,1,0:T(8,128)}, f32[2,128,3264]{1,2,0:T(8,128)}, ...) | async-done | bytes 17825808 | tf_op jit(solution)/shard_map/psum | solution.py:353
  (578 shorter events, 342.7 us)
Async XLA Ops:
  7.2 241.1 %all-reduce.14.cloned.1.call-start = ((), (), s32[]{:S(2)}) async-start(), calls=%async_computation.11 | async-start | bytes 37879808
  22.9 557.7 %all-gather.21.cloned.1.call-start = ((), (), s32[]{:S(2)}) async-start(), calls=%async_computation.6 | async-start | bytes 19087872 | tf_op jit(solution)/shard_map/all_gather | solution.py:192
  24.7 890.1 %all-gather.23.cloned.1.call-start = ((), (), s32[]{:S(2)}) async-start(), calls=%async_computation.7 | async-start | bytes 19087872 | tf_op jit(solution)/shard_map/all_gather | solution.py:193
  25.7 1107.8 %all-gather.17.cloned.1.call-start = ((), (), s32[]{:S(2)}) async-start(), calls=%async_computation.2 | async-start | bytes 9469952 | tf_op jit(solution)/shard_map/all_gather | solution.py:203
  26.4 1148.8 %copy-start.121 = (f32[1088]{0:T(1024)}, f32[1088]{0:T(1024)S(1)}, u32[]{:S(2)}) copy-start(f32[1088]{0:T(1024)S(1)} %get-tuple-element.158) | copy-start | bytes 13060
  26.4 1167.3 %copy-start.123 = (f32[1088]{0:T(1024)}, f32[1088]{0:T(1024)S(1)}, u32[]{:S(2)}) copy-start(f32[1088]{0:T(1024)S(1)} %get-tuple-element.160) | copy-start | bytes 13060
  26.5 221.8 %copy-start.129 = (f32[2,64]{1,0:T(2,128)}, f32[2,64]{1,0:T(2,128)S(1)}, u32[]{:S(2)}) copy-start(f32[2,64]{1,0:T(2,128)S(1)} %broadcast_multiply_fusion) | copy-start | bytes 1540
  27.8 239.9 %copy-start.93 = (bf16[128,128]{1,0:T(8,128)(2,1)}, bf16[128,128]{1,0:T(8,128)(2,1)S(1)}, u32[]{:S(2)}) copy-start(bf16[128,128]{1,0:T(8,128)(2,1)S(1)} %fusion.68) | copy-start | bytes 98308
  269.3 1055.3 %all-gather.25.cloned.1.call-start = ((), (), s32[]{:S(2)}) async-start(), calls=%async_computation.8 | async-start | bytes 19087872 | tf_op jit(solution)/shard_map/all_gather | solution.py:192
  269.9 1388.8 %all-gather.27.cloned.1.call-start = ((), (), s32[]{:S(2)}) async-start(), calls=%async_computation.9 | async-start | bytes 19087872 | tf_op jit(solution)/shard_map/all_gather | solution.py:193
  270.4 1616.9 %all-gather.19.cloned.1.call-start = ((), (), s32[]{:S(2)}) async-start(), calls=%async_computation.3 | async-start | bytes 9469952 | tf_op jit(solution)/shard_map/all_gather | solution.py:203
  283.5 891.2 %copy-start.6 = (f32[128,1088]{0,1:T(8,128)}, f32[128,1088]{0,1:T(8,128)S(1)}, u32[]{:S(2)}) copy-start(f32[128,1088]{0,1:T(8,128)S(1)} %copy.106) | copy-start | bytes 1671172
  289.8 883.7 %copy-start.2 = (bf16[1088,1088]{1,0:T(8,128)(2,1)}, bf16[1088,1088]{1,0:T(8,128)(2,1)S(1)}, u32[]{:S(2)}) copy-start(bf16[1088,1088]{1,0:T(8,128)(2,1)S(1)} %reshape.370) | copy-start | bytes 7102468
  1175.0 18.1 copy-start.4
  1176.0 13.0 slice-start.6
  1199.2 908.9 %reduce-scatter.3.cloned.1.call-start = ((), (), s32[]{:S(2)}) async-start(), calls=%async_computation.4 | async-start | bytes 9469952 | tf_op jit(solution)/shard_map/reduce_scatter | solution.py:311
  1929.1 17.5 copy-start.8
  1930.1 12.9 slice-start.3
  2004.0 283.1 %reduce-scatter.5.cloned.1.call-start = ((), (), s32[]{:S(2)}) async-start(), calls=%async_computation.5 | async-start | bytes 9469952 | tf_op jit(solution)/shard_map/reduce_scatter | solution.py:311
  2010.0 103.6 %copy-start.75 = (bf16[128,1088]{1,0:T(8,128)(2,1)}, bf16[128,1088]{1,0:T(8,128)(2,1)S(1)}, u32[]{:S(2)}) copy-start(bf16[128,1088]{1,0:T(8,128)(2,1)S(1)} %reshape.430) | copy-start | bytes 835588
  2183.3 338.5 %all-reduce.12.cloned.1.call-start = ((), (), s32[]{:S(2)}) async-start(), calls=%async_computation.10 | async-start | bytes 35651584 | tf_op jit(solution)/shard_map/psum | solution.py:353
  2199.7 9.9 copy-start.96
  2220.4 66.7 %copy-start.77 = (bf16[128,1088]{1,0:T(8,128)(2,1)S(1)}, bf16[128,1088]{1,0:T(8,128)(2,1)}, u32[]{:S(2)}) copy-start(bf16[128,1088]{1,0:T(8,128)(2,1)} %reshape.431) | copy-start | bytes 835588
  2521.8 10.1 slice-start.16
  (155 other events, 541.4 us)
Sparse Core Ops, SparseCore 0:
  23.0 225.2 all-reduce.13
  250.7 329.8 all-gather.20
  582.9 331.7 all-gather.22
  917.9 75.5 all-gather.16
  995.8 328.7 all-gather.24
  1326.8 331.7 all-gather.26
  1662.0 75.5 all-gather.18
  2004.1 103.9 reduce-scatter.2
  2183.4 103.6 reduce-scatter.4
  2298.5 223.2 all-reduce.11
where the time goes:
time: 2560 us; the launch traced here: 2550 us
  waiting for transfers between devices  1220 us (48%)
  other arithmetic  860 us (34%)
  local copies, waits for them, and re-layouts  251 us (10%)
  matrix products  183 us (7%)
    all_gather x2, other arithmetic, shards(): lax.all_gather(w_down[layer_idx], ('seq', 'batch'), axis=0, tiled=True)  403 us
    all_gather x2, other arithmetic, shards(): lax.all_gather(w_up[layer_idx], ('seq', 'batch'), axis=0, tiled=True)  403 us
    all_gather x2, waiting for transfers between devices, shards(): lax.all_gather(w_up[layer_idx], ('seq', 'batch'), axis=0, tiled=True)  397 us
    all_gather x2, waiting for transfers between devices, shards(): lax.all_gather(w_down[layer_idx], ('seq', 'batch'), axis=0, tiled=True)  230 us
    unnamed x11, waiting for transfers between devices  222 us
    psum x1, waiting for transfers between devices, shards(): lax.psum((stacked[0], stacked[1], stacked[2], stacked[3], stacked[4], sta...  212 us
    reduce_scatter x2, waiting for transfers between devices, shards(): lax.psum_scatter(jnp.concatenate([grad_keys.reshape(row_count, micro_coun...  162 us
    dot_general x24, matrix products, dot_plain(): return jnp.dot(left_side, right_side, preferred_element_type=jnp.float32)  55.4 us
  transfers between devices with their start and end apart: 10, of which 8 were waited for; matrix products, arithmetic and copies ran while one was open for 41% of the time, Pallas kernels for 0%

commit v1 on v0

v1 whole, which is shorter than its diff:
```python
import jax
import jax.numpy as jnp
from jax import lax
from jax.experimental import pallas as pl
from jax.experimental.pallas import tpu as pltpu
from jax.sharding import PartitionSpec as P

D = 1088
HEADS = 17
HEAD_DIM = 64
FF = 4352
RANK = 16
WIDE = 1152
PAIRS = 9
HALF = 64
KEYS = 1024
BF = jnp.bfloat16
F32 = jnp.float32
NEG = -1e30

SWAP = [(i, i ^ 8) for i in range(16)]
CORE = [(i, i ^ 1) for i in range(16)]
UP = [(i, (i & 8) | ((i + 2) & 7)) for i in range(16)]
DOWN = [(i, (i & 8) | ((i - 2) & 7)) for i in range(16)]
def at_chip(z, y, x, core):
    return ((z // 2 * 4 + y) * 2 + core) * 8 + x * 2 + z % 2


ALL = [[at_chip(z, y, x, c) for z in range(4) for y in range(4) for x in range(4) for c in range(2)]]
SAME_SEQUENCE = [[at_chip(z, y, x, c) for y in range(4) for c in range(2)] for z in range(4) for x in range(4)]
SAME_PLACE = [[at_chip(z, y, x, c) for z in range(4) for x in range(4)] for y in range(4) for c in range(2)]


def z_shift(by):
    return [
        (at_chip(z, y, x, c), at_chip((z + by) % 4, y, x, c))
        for z in range(4) for y in range(4) for x in range(4) for c in range(2)
    ]


def x_shift(by):
    return [(i, (i + 2 * by) % 8) for i in range(8)]


BOTH = ("seq", "batch")
TURNED = (D, D, D, FF, 3 * D, D, D)
PART_A, PART_B = 1664, 640
PART = PART_A + PART_B

LINES = 304
AT_OUT = 224
N_QKV, N_OUT, N_UP, N_DOWN = 217, 73, 289, 289
BLOCK = 136


def dot(a, b):
    return jnp.dot(a, b, preferred_element_type=F32)


def dot_t(a, b):
    return lax.dot_general(a, b, (((1,), (1,)), ((), ())), preferred_element_type=F32)


def t_dot(a, b):
    return lax.dot_general(a, b, (((0,), (0,)), ((), ())), preferred_element_type=F32)


def norm_stats(v):
    mean = jnp.mean(v, axis=-1, keepdims=True)
    centred = v - mean
    inv = lax.rsqrt(jnp.mean(centred * centred, axis=-1, keepdims=True) + 1e-05)
    return centred * inv, inv


def norm_back(v, gain, grad):
    r, inv = norm_stats(v)
    gr = grad * gain
    return inv * (
        gr - jnp.mean(gr, axis=-1, keepdims=True) - r * jnp.mean(gr * r, axis=-1, keepdims=True)
    )


def widen(a):
    return jnp.pad(a, ((0, 0), (0, WIDE - D)))


def lanes(rows):
    return lax.broadcasted_iota(jnp.int32, (rows, 128), 1)


def two_heads(block):
    low = lanes(block.shape[0]) < HEAD_DIM
    zero = jnp.zeros_like(block)
    return jnp.concatenate([jnp.where(low, block, zero), jnp.where(low, zero, block)], axis=0)


def one_block(stacked):
    rows = stacked.shape[0] // 2
    return jnp.where(lanes(rows) < HEAD_DIM, stacked[:rows], stacked[rows:])


def pick_extra(rows, pair):
    spot = lanes(rows) - HEAD_DIM
    head = 2 * pair

    def of(h):
        return ((spot >= 3 * h) & (spot < 3 * h + 3)).astype(F32)

    return jnp.concatenate([of(head), of(head + 1)], axis=0)


def gathered(own_ref, sib_ref, half):
    width = own_ref.shape[-1]
    return jnp.concatenate(
        [own_ref[:, half].reshape(4 * HALF, width), sib_ref[:, half].reshape(4 * HALF, width)],
        axis=0,
    )


def row_terms(term):
    first = term.astype(BF).astype(F32)
    rest = term - first
    second = rest.astype(BF).astype(F32)
    third = rest - second
    turn = (lanes(term.shape[0]) - HEAD_DIM) % 3
    return jnp.where(turn == 0, first, jnp.where(turn == 1, second, third)).astype(BF)


def fwd_kernel(
    q_ref, ko_ref, ks_ref, vo_ref, vs_ref, lpos, lseg, kpos, kseg, ctx_ref, qe_ref, b_lo, b_hi, acc
):
    pair = pl.program_id(0)

    @pl.when(pair == 0)
    def _():
        ok = (kpos[...] <= lpos[...]) & (kseg[...] == lseg[...])
        bias = jnp.where(ok, 0.0, NEG)
        lo = bias[:HALF, : KEYS // 2]
        hi = bias[HALF:]
        b_lo[...] = jnp.concatenate([lo, lo], axis=0)
        b_hi[...] = jnp.concatenate([hi, hi], axis=0)
        acc[...] = jnp.zeros_like(acc)

    q = q_ref[...]
    k_lo = gathered(ko_ref, ks_ref, 0)
    k_hi = gathered(ko_ref, ks_ref, 1)
    v_lo = gathered(vo_ref, vs_ref, 0)
    v_hi = gathered(vo_ref, vs_ref, 1)
    spot = lanes(HALF) - HEAD_DIM
    head = 2 * pair

    def attend(rows, keys, values, bias, at):
        s = dot_t(two_heads(rows), keys) + bias
        top = jnp.max(s, axis=1, keepdims=True)
        e = jnp.exp(s - top)
        total = jnp.sum(e, axis=1, keepdims=True)
        p = (e * (1.0 / total)).astype(BF)
        ctx_ref[pl.ds(at, HALF), :] = one_block(dot(p, values)).astype(BF)
        lse = top + jnp.log(total)
        old = acc[pl.ds(at, HALF), :]
        new = jnp.where((spot >= 3 * head) & (spot < 3 * head + 3), -lse[:HALF], old)
        new = jnp.where((spot >= 3 * head + 3) & (spot < 3 * head + 6), -lse[HALF:], new)
        acc[pl.ds(at, HALF), :] = new

    attend(q[:HALF], k_lo, v_lo, b_lo[...], 0)
    attend(
        q[HALF:],
        jnp.concatenate([k_lo, k_hi], axis=0),
        jnp.concatenate([v_lo, v_hi], axis=0),
        b_hi[...],
        HALF,
    )
    qe_ref[...] = q

    @pl.when(pair == PAIRS - 1)
    def _():
        where = lanes(2 * HALF)
        keep = (where >= HEAD_DIM) & (where < HEAD_DIM + 3 * HEADS)
        extra = jnp.where(keep, row_terms(acc[...]), jnp.zeros((2 * HALF, 128), BF))
        qe_ref[...] = jnp.where(where < HEAD_DIM, q, extra)


def dq_kernel(
    qe_ref, ge_ref, qx_ref, gx_ref, ko_ref, ks_ref, vo_ref, vs_ref, lpos, lseg, kpos, kseg,
    gq_ref, b_lo, b_hi
):
    pair = pl.program_id(0)

    @pl.when(pair == 0)
    def _():
        ok = (kpos[...] <= lpos[...]) & (kseg[...] == lseg[...])
        bias = jnp.where(ok, 0.0, NEG)
        lo = bias[:HALF, : KEYS // 2]
        hi = bias[HALF:]
        b_lo[...] = jnp.concatenate([lo, lo], axis=0)
        b_hi[...] = jnp.concatenate([hi, hi], axis=0)

    k_lo = gathered(ko_ref, ks_ref, 0)
    k_hi = gathered(ko_ref, ks_ref, 1)
    v_lo = gathered(vo_ref, vs_ref, 0)
    v_hi = gathered(vo_ref, vs_ref, 1)
    low = lanes(HALF) < HEAD_DIM
    last = pair == PAIRS - 1

    def with_terms(rows, extra):
        rows = jnp.where(last & ~low, jnp.zeros_like(rows), rows)
        mask = pick_extra(HALF, pair).astype(BF)
        both = jnp.concatenate([extra, extra], axis=0) * mask
        return jnp.concatenate([two_heads(rows), both], axis=1)

    def back(at, keys, values, bias):
        ones = jnp.ones((keys.shape[0], 128), BF)
        q = with_terms(qe_ref[pl.ds(at, HALF), :], qx_ref[pl.ds(at, HALF), :])
        g = with_terms(ge_ref[pl.ds(at, HALF), :], gx_ref[pl.ds(at, HALF), :])
        s = dot_t(q, jnp.concatenate([keys, ones], axis=1)) + bias
        dp = dot_t(g, jnp.concatenate([values, ones], axis=1))
        ds = (jnp.exp(s) * dp).astype(BF)
        gq_ref[pl.ds(at, HALF), :] = (one_block(dot(ds, keys)) * 0.125).astype(BF)

    back(0, k_lo, v_lo, b_lo[...])
    back(
        HALF,
        jnp.concatenate([k_lo, k_hi], axis=0),
        jnp.concatenate([v_lo, v_hi], axis=0),
        b_hi[...],
    )


def dkv_kernel(
    k_ref, v_ref, qo_ref, qs_ref, go_ref, gs_ref, qxo_ref, qxs_ref, gxo_ref, gxs_ref,
    lpos, lseg, kpos, kseg, gk_ref, gv_ref, b_lo, b_hi
):
    pair = pl.program_id(0)

    @pl.when(pair == 0)
    def _():
        ok = (lpos[...] <= kpos[...]) & (kseg[...] == lseg[...])
        bias = jnp.where(ok, 0.0, NEG)
        lo = bias[:HALF]
        hi = bias[HALF:, KEYS // 2 :]
        b_lo[...] = jnp.concatenate([lo, lo], axis=0)
        b_hi[...] = jnp.concatenate([hi, hi], axis=0)

    low = lanes(HALF) < HEAD_DIM
    last = pair == PAIRS - 1
    q_lo, q_hi = gathered(qo_ref, qs_ref, 0), gathered(qo_ref, qs_ref, 1)
    g_lo, g_hi = gathered(go_ref, gs_ref, 0), gathered(go_ref, gs_ref, 1)
    qx_lo, qx_hi = gathered(qxo_ref, qxs_ref, 0), gathered(qxo_ref, qxs_ref, 1)
    gx_lo, gx_hi = gathered(gxo_ref, gxs_ref, 0), gathered(gxo_ref, gxs_ref, 1)
    terms = pick_extra(HALF, pair).astype(BF)

    def back(half, q, g, qx, gx, bias):
        k = jnp.concatenate([two_heads(k_ref[half]), terms], axis=1)
        v = jnp.concatenate([two_heads(v_ref[half]), terms], axis=1)
        p = jnp.exp(dot_t(k, jnp.concatenate([q, qx], axis=1)) + bias)
        dp = dot_t(v, jnp.concatenate([g, gx], axis=1))
        ds = (p * dp).astype(BF)
        gk = one_block(dot(ds, q)).astype(BF)
        gv = one_block(dot(p.astype(BF), g)).astype(BF)
        drop = last & ~low
        gk_ref[half] = jnp.where(drop, jnp.zeros_like(gk), gk)
        gv_ref[half] = jnp.where(drop, jnp.zeros_like(gv), gv)

    def both(a, b):
        return jnp.concatenate([a, b], axis=0)

    back(0, both(q_lo, q_hi), both(g_lo, g_hi), both(qx_lo, qx_hi), both(gx_lo, gx_hi), b_lo[...])
    back(1, q_hi, g_hi, qx_hi, gx_hi, b_hi[...])


def spec_rows(at):
    return pl.BlockSpec((2 * HALF, 128), lambda i: (0, at(i)))


def spec_all(at):
    return pl.BlockSpec((4, 2, HALF, 128), lambda i: (0, 0, 0, at(i)))


def spec_half(at):
    return pl.BlockSpec((2, HALF, 128), lambda i: (0, 0, at(i)))


def same(i):
    return i


def value_at(i):
    return i + PAIRS


def last_at(i):
    return PAIRS - 1


def spec_whole(shape):
    return pl.BlockSpec(shape, lambda i: (0, 0))


MASK_SPECS = [
    spec_whole((2 * HALF, 1)),
    spec_whole((2 * HALF, 1)),
    spec_whole((1, KEYS)),
    spec_whole((1, KEYS)),
]
BIAS_SCRATCH = [
    pltpu.VMEM((2 * HALF, KEYS // 2), F32),
    pltpu.VMEM((2 * HALF, KEYS), F32),
]
BIAS_SCRATCH_T = [
    pltpu.VMEM((2 * HALF, KEYS), F32),
    pltpu.VMEM((2 * HALF, KEYS // 2), F32),
]
PARAMS = pltpu.CompilerParams(vmem_limit_bytes=32 * 1024 * 1024)
FLAT = jax.ShapeDtypeStruct((2 * HALF, WIDE), BF)


def attend_fwd(q, kv_own, kv_sib, where):
    return pl.pallas_call(
        fwd_kernel,
        grid=(PAIRS,),
        out_shape=(FLAT, FLAT),
        in_specs=[spec_rows(same), spec_all(same), spec_all(same), spec_all(value_at)]
        + [spec_all(value_at)]
        + MASK_SPECS,
        out_specs=(spec_rows(same), spec_rows(same)),
        scratch_shapes=BIAS_SCRATCH + [pltpu.VMEM((2 * HALF, 128), F32)],
        compiler_params=PARAMS,
        cost_estimate=pl.CostEstimate(
            flops=PAIRS * 4 * 256 * KEYS * 128, bytes_accessed=6 << 20, transcendentals=PAIRS * 256 * KEYS
        ),
    )(q, kv_own, kv_sib, kv_own, kv_sib, *where)


def attend_dq(qe, ge, kv_own, kv_sib, where):
    return pl.pallas_call(
        dq_kernel,
        grid=(PAIRS,),
        out_shape=FLAT,
        in_specs=[spec_rows(same), spec_rows(same), spec_rows(last_at), spec_rows(last_at)]
        + [spec_all(same), spec_all(same), spec_all(value_at), spec_all(value_at)]
        + MASK_SPECS,
        out_specs=spec_rows(same),
        scratch_shapes=BIAS_SCRATCH,
        compiler_params=PARAMS,
        cost_estimate=pl.CostEstimate(
            flops=PAIRS * 8 * 256 * KEYS * 128, bytes_accessed=6 << 20, transcendentals=PAIRS * 256 * KEYS
        ),
    )(qe, ge, qe, ge, kv_own, kv_sib, kv_own, kv_sib, *where)


def attend_dkv(kv, qe_own, qe_sib, ge_own, ge_sib, where):
    part = jax.ShapeDtypeStruct((2, HALF, WIDE), BF)
    return pl.pallas_call(
        dkv_kernel,
        grid=(PAIRS,),
        out_shape=(part, part),
        in_specs=[spec_half(same), spec_half(value_at)]
        + [spec_all(same)] * 4
        + [spec_all(last_at)] * 4
        + MASK_SPECS,
        out_specs=(spec_half(same), spec_half(same)),
        scratch_shapes=BIAS_SCRATCH_T,
        compiler_params=PARAMS,
        cost_estimate=pl.CostEstimate(
            flops=PAIRS * 12 * 256 * KEYS * 128, bytes_accessed=6 << 20, transcendentals=PAIRS * 256 * KEYS
        ),
    )(kv, kv, qe_own, qe_sib, ge_own, ge_sib, qe_own, qe_sib, ge_own, ge_sib, *where)


def ring_start(block):
    return lax.ppermute(block, "seq", UP), lax.ppermute(block, "seq", DOWN)


def ring_far(block, before, after):
    far_lo = lax.ppermute(before[0], "seq", UP)
    far_hi = lax.ppermute(after[1], "seq", DOWN)
    return jnp.stack([block, before, after, jnp.stack([far_lo, far_hi])])


def other_core(own):
    return lax.ppermute(own, "seq", CORE)


def tie(*values):
    return lax.optimization_barrier(values)


def eighths(turned, straight):
    def cut(a, part):
        return jnp.pad(a, ((0, 0), (0, 8 * part - a.shape[1]))).reshape(RANK, 8, part)

    first = cut(jnp.concatenate(turned, axis=1), PART_A)
    return jnp.swapaxes(jnp.concatenate([first, cut(straight, PART_B)], axis=2), 0, 1)


def by_adapter_kernel(picks, *refs):
    parts, out_ref, acc = refs[:-2], refs[-2], refs[-1]
    acc[...] = jnp.zeros_like(acc)
    at = 0
    for ref in parts:
        for k in range(ref.shape[0]):
            rows = pl.ds(pl.multiple_of(picks[at] * RANK, RANK), RANK)
            acc[rows, :] = acc[rows, :] + ref[k].astype(F32)
            at += 1
    for j in range(PART // 128):
        square = acc[:, 128 * j : 128 * (j + 1)]
        square = square.T if 128 * j < PART_A else square
        out_ref[128 * j : 128 * (j + 1), :] = square.astype(BF)


def by_adapter(parts, picks):
    return pl.pallas_call(
        by_adapter_kernel,
        out_shape=jax.ShapeDtypeStruct((PART, 128), BF),
        in_specs=[pl.BlockSpec(memory_space=pltpu.SMEM)]
        + [pl.BlockSpec(memory_space=pltpu.VMEM)] * len(parts),
        out_specs=pl.BlockSpec(memory_space=pltpu.VMEM),
        scratch_shapes=[pltpu.VMEM((8 * RANK, PART), F32)],
        compiler_params=PARAMS,
        cost_estimate=pl.CostEstimate(flops=16 * RANK * PART, bytes_accessed=2 << 20, transcendentals=0),
    )(picks, *parts)


def unfold_kernel(place, own_ref, sib_ref, one_ref, *outs):
    turned, straight = outs[:-1], outs[-1]

    def rows(layer, e, at, n):
        if layer == 1:
            return one_ref[e, at : at + n, :].astype(F32)
        k = place[e]
        mine = own_ref[k % 4, at : at + n, :]
        other = sib_ref[k % 4, at : at + n, :]
        return jnp.where(k < 4, mine.astype(F32), other.astype(F32))

    for layer in range(2):
        start = 0
        for out, width in zip(turned, TURNED):
            at = start
            while at < start + width:
                n = min(start + width, (at // PART_A + 1) * PART_A) - at
                out[layer, at - start : at - start + n, :] = rows(layer, at // PART_A, at % PART_A, n)
                at += n
            start += width
        squares = PART_B // 128
        for t in range(FF // 128):
            value = rows(layer, t // squares, PART_A + 128 * (t % squares), 128)
            straight[layer, :, 128 * t : 128 * (t + 1)] = value


def unfold(own, sib, one, place):
    shapes = [(2, w, 128) for w in TURNED] + [(2, 128, FF)]
    whole = pl.BlockSpec(memory_space=pltpu.VMEM)
    return pl.pallas_call(
        unfold_kernel,
        out_shape=tuple(jax.ShapeDtypeStruct(shape, F32) for shape in shapes),
        in_specs=[pl.BlockSpec(memory_space=pltpu.SMEM), whole, whole, whole],
        out_specs=(whole,) * 8,
        compiler_params=pltpu.CompilerParams(vmem_limit_bytes=56 * 1024 * 1024),
        cost_estimate=pl.CostEstimate(flops=0, bytes_accessed=28 << 20, transcendentals=0),
    )(place, own, sib, one)


def share(w_qkv, w_out, w_up, w_down, z_lo):
    def half_row(w, front, lines):
        size = lines * 128 - w.shape[1]
        first = jnp.pad(w, ((0, 0), (0, size)))
        second = jnp.pad(w, ((0, 0), (front, size - front)))
        return jnp.where(z_lo == 0, first, second).reshape(-1, lines, 128)

    def put(a, room):
        return jnp.pad(a, ((0, 0), (0, room - a.shape[1]), (0, 0)))

    attention = [
        put(half_row(w_qkv, 32, N_QKV), AT_OUT),
        put(half_row(w_out, 32, N_OUT), LINES - AT_OUT),
    ]
    up, down = put(w_up.reshape(-1, N_UP, 128), LINES), put(w_down.reshape(-1, N_DOWN, 128), LINES)
    return jnp.concatenate(attention, axis=1), jnp.concatenate([up, down], axis=1)


def spin(a):
    return pltpu.roll(a, HEAD_DIM, 1)


def fill(ref, base, lines):
    ref[pl.ds(base, lines.shape[0], stride=2), :] = lines


def between(ref, base, n):
    now, later = ref[pl.ds(base, n, stride=2), :], ref[pl.ds(base + 2, n, stride=2), :]
    ref[pl.ds(base + 1, n, stride=2), :] = spin(jnp.where(lanes(n) < HEAD_DIM, later, now))


def columns(ref, dst, to, start, units, step=2):
    got = ref[pl.ds(start, dst.shape[0], stride=units), :].astype(BF)
    n = min(128, dst.shape[1] - to)
    dst[:, to : to + n] = got[:, :n]


def lines_of(ref, pair, zl, start, n):
    return ref[0, zl, 0, pair % 4, pair // 4, start : start + n, :].astype(F32)


def unpack_attention_kernel(g_ref, q_ref, kv_ref, out_ref, s_qkv, s_out):
    low = lanes(1) < HEAD_DIM
    zero = jnp.zeros((1, 128), F32)
    for pair in range(8):
        qkv0, qkv1 = (lines_of(g_ref, pair, zl, 0, N_QKV) for zl in range(2))
        out0, out1 = (lines_of(g_ref, pair, zl, AT_OUT, N_OUT) for zl in range(2))
        base, base_out = pair * 867, pair * 289
        fill(s_qkv, base, qkv0)
        fill(s_qkv, base + 433, qkv1)
        between(s_qkv, base, N_QKV - 1)
        between(s_qkv, base + 433, N_QKV)
        s_qkv[pl.ds(base + 432, 1), :] = qkv0[N_QKV - 1 :] + spin(jnp.where(low, qkv1[:1], zero))
        s_qkv[pl.ds(base + 433, 1), :] = qkv1[:1] + spin(jnp.where(low, zero, qkv0[N_QKV - 1 :]))
        fill(s_out, base_out, out0)
        fill(s_out, base_out + 144, out1)
        s_out[pl.ds(base_out + 144, 1), :] = out0[N_OUT - 1 :] + out1[:1]
        between(s_out, base_out, N_OUT - 1)
        between(s_out, base_out + 144, N_OUT - 1)
    half = lanes(BLOCK) < HEAD_DIM
    for dst, to, first in ((q_ref, 0, 0), (kv_ref, 0, 17), (kv_ref, WIDE, 34)):
        for j in range(8):
            columns(s_qkv, dst, to + 128 * j, first + 2 * j, 51)
        got = s_qkv[pl.ds(first + 16, BLOCK, stride=51), :]
        dst[:, to + D - HEAD_DIM : to + WIDE] = jnp.where(half, got, 0.0).astype(BF)
    for j in range(9):
        columns(s_out, out_ref, 128 * j, 2 * j, 17)


def unpack_mlp_kernel(g_up, g_down, up_ref, down_ref, s_up, s_down):
    for pair in range(8):
        for zl in range(2):
            at = pair * 2 + zl
            s_up[pl.ds(at * N_UP, N_UP), :] = lines_of(g_up, pair, zl, 0, N_UP)
            fill(s_down, at * 2 * N_DOWN, lines_of(g_down, pair, zl, 0, N_DOWN))
    for at in range(16):
        between(s_down, at * 2 * N_DOWN, N_DOWN)
    for j in range(34):
        columns(s_up, up_ref, 128 * j, j, 34)
    for j in range(9):
        columns(s_down, down_ref, 128 * j, 2 * j, 17)


def unpack(kernel, got, at, outs, scratch_lines):
    g = got.reshape(2, 2, 4, 4, 2, -1, 128)

    def spec(k):
        return pl.BlockSpec((1, 2, 1, 4, 2, LINES, 128), lambda i: (i // 4, 0, i % 4, 0, 0, k, 0))

    return pl.pallas_call(
        kernel,
        grid=(8,),
        out_shape=tuple(jax.ShapeDtypeStruct((8 * r, w), BF) for r, w in outs),
        in_specs=[spec(k) for k in at],
        out_specs=tuple(pl.BlockSpec((r, w), lambda i: (i, 0)) for r, w in outs),
        scratch_shapes=[pltpu.VMEM((n, 128), F32) for n in scratch_lines],
        compiler_params=pltpu.CompilerParams(vmem_limit_bytes=48 * 1024 * 1024),
        cost_estimate=pl.CostEstimate(
            flops=0, bytes_accessed=len(at) * (20 << 20), transcendentals=0
        ),
    )(*[g] * len(at))


def unpack_attention(got, at):
    outs = [(BLOCK, WIDE), (BLOCK, 2 * WIDE), (BLOCK, D)]
    return unpack(unpack_attention_kernel, got, [at], outs, [8 * 867 + 8, 8 * 289 + 8])


def unpack_mlp(got, at):
    outs = [(BLOCK, FF), (4 * BLOCK, D)]
    return unpack(unpack_mlp_kernel, got, [at, at + 1], outs, [16 * N_UP, 32 * N_DOWN + 8])


def shards(
    tokens, segments, adapter_pick, norm_gain, w_qkv, w_out, w_up, w_down,
    a_qkv, b_qkv, a_out, b_out, a_up, b_up, a_down, b_down, grad_out
):
    layers = norm_gain.shape[0]
    index = lax.axis_index("seq")
    z_hi, place = index // 8, index % 8
    core, y = place % 2, place // 2

    attention, mlp = share(w_qkv, w_out, w_up, w_down, lax.axis_index("batch") % 2)

    def gather(a):
        return lax.all_gather(a, BOTH, axis=0, tiled=True, axis_index_groups=ALL)

    early = gather(jnp.concatenate([attention[0], mlp[0], attention[1]], axis=0))
    late = gather(mlp[1])

    def halves(own, other):
        return jnp.where(z_hi == 0, jnp.stack([own, other]), jnp.stack([other, own]))

    def mine(a):
        return lax.dynamic_index_in_dim(a, z_hi, 0, keepdims=False)

    def theirs(a):
        return lax.dynamic_index_in_dim(a, 1 - z_hi, 0, keepdims=False)

    sent = lax.ppermute(jnp.stack([theirs(tokens), theirs(grad_out)]), "seq", SWAP)
    hidden = halves(mine(tokens), sent[0]).reshape(2 * HALF, D).astype(F32)
    grad_hidden = halves(mine(grad_out), sent[1]).reshape(2 * HALF, D).astype(F32)
    pick = mine(adapter_pick)

    row = jnp.zeros((2, KEYS), jnp.int32)
    row = lax.dynamic_update_slice(row, segments, (0, index * HALF))
    seg = mine(lax.psum(row, "seq")).reshape(2, 8, HALF)
    offset = jnp.arange(HALF, dtype=jnp.int32)
    start = jnp.array([0, KEYS // 2], jnp.int32)[:, None]
    lpos = (start + place * HALF + offset[None]).reshape(2 * HALF, 1)
    lseg = lax.dynamic_index_in_dim(seg, place, 1, keepdims=False).reshape(2 * HALF, 1)
    ys = (y + jnp.array([0, 3, 1, 2], jnp.int32)) % 4
    order = jnp.concatenate([2 * ys + core, 2 * ys + 1 - core])
    kpos = (start[:, :, None] + (order * HALF)[None, :, None] + offset).reshape(1, KEYS)
    kseg = jnp.take(seg, order, axis=1).reshape(1, KEYS)
    where = (lpos, lseg, kpos, kseg)

    steps = jnp.array([0, 3, 1, 2], jnp.int32)
    batch = lax.axis_index("batch")
    z, x = z_hi * 2 + batch % 2, batch // 2
    picks = lax.dynamic_update_slice(jnp.zeros((16,), jnp.int32), adapter_pick, (2 * batch,))
    picks = lax.psum(picks, "batch")

    picks, where, hidden = lax.optimization_barrier((picks, where, hidden))

    def sequence(zs, xs):
        return 2 * (2 * xs + zs % 2) + zs // 2

    four = jnp.arange(4, dtype=jnp.int32)
    picks_in_order = jnp.take(picks, sequence(four[:, None], four[None, :]).reshape(16))
    zs, xs = (z + steps) % 4, (x + steps) % 4
    picks_by_step = jnp.take(picks, sequence(zs[None, :], xs[:, None]).reshape(16))
    eight = jnp.arange(8, dtype=jnp.int32)
    back = jnp.array([0, 2, 3, 1], jnp.int32)
    place_by_step = 4 * ((eight % 2) ^ core) + jnp.take(back, (eight // 2 - y) % 4)

    def low_in(a, l):
        return lax.dynamic_slice_in_dim(a[l], pick * RANK, RANK, 1)

    def low_out(b, l):
        return lax.dynamic_slice_in_dim(b[l], pick * RANK, RANK, 0)

    def project(x, w, a, b):
        low = dot(x, a).astype(BF)
        return dot(x, w) + dot(low, b), low

    def pull(gz, x, low, w, a, b):
        glow = dot_t(gz, b).astype(BF)
        return dot_t(gz, w) + dot_t(glow, a), t_dot(glow, x), t_dot(low, gz)

    saved = []
    first = unpack_attention(early, 0)
    for l in range(layers):
        a_first = low_in(a_qkv, l)
        b_first = low_out(b_qkv, l)
        b_q = widen(b_first[:, :D])
        b_kv = jnp.concatenate([widen(b_first[:, D : 2 * D]), widen(b_first[:, 2 * D :])], axis=1)
        ad = [(low_in(a, l), low_out(b, l)) for a, b in ((a_out, b_out), (a_up, b_up), (a_down, b_down))]
        wq, wkv, wout = first
        n1 = (norm_stats(hidden)[0] * norm_gain[l, 0]).astype(BF)
        low_qkv = dot(n1, a_first).astype(BF)
        kv = (dot(n1, wkv) + dot(low_qkv, b_kv)).astype(BF).reshape(2, HALF, 2 * WIDE)
        before, after = ring_start(kv)
        q = (dot(n1, wq) + dot(low_qkv, b_q)).astype(BF) * jnp.asarray(0.125, BF)
        wup, wdown = unpack_mlp(early, 1) if l == 0 else unpack_mlp(late, 0)
        before, after, q, wup, wdown = tie(before, after, q, wup, wdown)
        kv_own = ring_far(kv, before, after)
        if l == 0:
            first = unpack_attention(early, 3)
            kv_own, *first = tie(kv_own, *first)
        kv_sib = other_core(kv_own)
        ctx, qe = attend_fwd(q, kv_own, kv_sib, where)
        ctx = ctx[:, :D]
        qe = qe.reshape(2, HALF, WIDE)
        q_before, q_after = ring_start(qe)
        proj, low_o = project(ctx, wout, *ad[0])
        middle = hidden + proj
        n2 = (norm_stats(middle)[0] * norm_gain[l, 1]).astype(BF)
        up, low_u = project(n2, wup, *ad[1])
        act = jax.nn.gelu(up, approximate=False).astype(BF)
        q_before, q_after, act = tie(q_before, q_after, act)
        qe_own = ring_far(qe, q_before, q_after)
        y_out, low_d = project(act, wdown, *ad[2])
        qe_own, y_out = tie(qe_own, y_out)
        qe_sib = other_core(qe_own)
        saved.append((hidden, n1, low_qkv, kv, kv_own, kv_sib, qe.reshape(2 * HALF, WIDE), qe_own, qe_sib, ctx, low_o, middle, n2, low_u, up, act, low_d, ad, a_first, b_q, b_kv, wq, wkv, wout, wup, wdown))
        hidden = middle + y_out

    heads_of = (jnp.arange(D, dtype=jnp.int32) // HEAD_DIM)[:, None]
    spot = jnp.arange(HEAD_DIM, dtype=jnp.int32)[None, :]
    spread = (heads_of == spot // 3).astype(F32)

    behind = None
    g = grad_hidden
    for l in reversed(range(layers)):
        (hidden_in, n1, low_qkv, kv, kv_own, kv_sib, qe, qe_own, qe_sib, ctx, low_o, middle, n2, low_u, up, act, low_d, ad, a_first, b_q, b_kv, wq, wkv, wout, wup, wdown) = saved[l]
        gact, ga_d, gb_d = pull(g.astype(BF), act, low_d, wdown, *ad[2])
        gup = jax.vjp(lambda v: jax.nn.gelu(v, approximate=False), up)[1](gact)[0].astype(BF)
        gn2, ga_u, gb_u = pull(gup, n2, low_u, wup, *ad[1])
        gh2 = g + norm_back(middle, norm_gain[l, 1], gn2)
        gctx, ga_o, gb_o = pull(gh2.astype(BF), ctx, low_o, wout, *ad[0])
        gctx = gctx.astype(BF)
        delta = -jnp.dot(
            gctx.astype(F32) * ctx.astype(F32), spread, precision=lax.Precision.HIGHEST
        )
        d1 = delta.astype(BF).astype(F32)
        d2 = (delta - d1).astype(BF).astype(F32)
        terms = jnp.where(spot % 3 == 0, d1, jnp.where(spot % 3 == 1, d2, delta - d1 - d2)).astype(BF)
        ge = jnp.concatenate([gctx, terms], axis=1)
        g_block = ge.reshape(2, HALF, WIDE)
        g_before, g_after = ring_start(g_block)
        if behind is not None:
            behind, ge = tie(behind, ge)
            behind = lax.all_gather(behind.astype(BF), BOTH, axis=0, axis_index_groups=SAME_PLACE)
        gq = attend_dq(qe, ge, kv_own, kv_sib, where)
        g_before, g_after, gq = tie(g_before, g_after, gq)
        ge_own = ring_far(g_block, g_before, g_after)
        gb_q, gx_q, glow_q = t_dot(low_qkv, gq), dot_t(gq, wq), dot_t(gq, b_q)
        ge_own, ga_d, gb_d, ga_u, gb_u, ga_o, gb_o, gb_q, gx_q, glow_q = tie(
            ge_own, ga_d, gb_d, ga_u, gb_u, ga_o, gb_o, gb_q, gx_q, glow_q
        )
        ge_sib = other_core(ge_own)
        gk, gv = attend_dkv(kv, qe_own, qe_sib, ge_own, ge_sib, where)
        gkv = jnp.concatenate([gk, gv], axis=2).reshape(2 * HALF, 2 * WIDE)
        glow = (glow_q + dot_t(gkv, b_kv)).astype(BF)
        ga_q, gb_kv = t_dot(glow, n1), t_dot(low_qkv, gkv)
        gb_q = [gb_q[:, :D], gb_kv[:, :D], gb_kv[:, WIDE : WIDE + D]]
        parts = eighths([ga_q, ga_o, ga_u, ga_d] + gb_q + [gb_o, gb_d], gb_u)
        if l == 0:
            got = lax.all_to_all(parts.astype(BF), BOTH, 0, 0, axis_index_groups=SAME_SEQUENCE)
            part = jnp.sum(got.astype(F32), axis=0).astype(BF)
            along_z = jnp.stack([part] + [lax.ppermute(part, BOTH, z_shift(by)) for by in (1, -1, 2)])
            behind, along_z = tie(behind, along_z)
            behind = by_adapter([behind], picks_in_order)
            one = lax.all_gather(behind, BOTH, axis=0, axis_index_groups=SAME_SEQUENCE)
            before = lax.ppermute(along_z, "batch", x_shift(1))
            after = lax.ppermute(along_z, "batch", x_shift(-1))
            far = [lax.ppermute(before[:2], "batch", x_shift(1)), lax.ppermute(after[2:], "batch", x_shift(-1))]
            whole = by_adapter([along_z, before, after] + far, picks_by_step)
            whole = whole.reshape(2, -1, 128)
            own = ring_far(whole, *ring_start(whole))
            sib = other_core(own).reshape(4, PART, 128)
            ga_q, ga_o, ga_u, ga_d, gb_q, gb_o, gb_d, gb_u = unfold(
                own.reshape(4, PART, 128), sib, one, place_by_step
            )
            gb_q, gb_o, gb_d = (jnp.swapaxes(a, 1, 2) for a in (gb_q, gb_o, gb_d))
        gn1 = gx_q + dot_t(gkv, wkv) + dot_t(glow, a_first)
        g = gh2 + norm_back(hidden_in, norm_gain[l, 0], gn1)
        if l > 0:
            parts, g = tie(parts, g)
            behind = lax.psum_scatter(
                parts, BOTH, scatter_dimension=0, axis_index_groups=SAME_SEQUENCE, tiled=True
            ).reshape(RANK, PART)

    def home(a):
        a = a.reshape(2, HALF, D)
        got = lax.ppermute(theirs(a), "seq", SWAP)
        return halves(mine(a), got)

    result, grad_tokens = home(hidden.astype(BF)), home(g)

    return result, grad_tokens, ga_q, gb_q, ga_o, gb_o, ga_u, gb_u, ga_d, gb_d


def solution(mesh):
    rows, flat, whole = P("batch", "seq", None), P(None, ("seq", "batch")), P()
    in_specs = (rows, P("batch", "seq"), P("batch"), whole) + (flat,) * 4 + (whole,) * 8 + (rows,)
    out_specs = (rows, rows) + (whole,) * 8
    return jax.shard_map(shards, mesh=mesh, in_specs=in_specs, out_specs=out_specs, check_vma=False)
```

time: 2560 us -> 625 us (0.24)
  waiting for transfers between devices: 1220 us -> 176 us
  other arithmetic: 860 us -> 33.6 us
  local copies, waits for them, and re-layouts: 251 us -> 41 us
  Pallas kernels: 0 us -> 144 us
  matrix products: 183 us -> 113 us
  starting transfers between devices: 0.79 us -> 70.7 us
    all_gather x4 -> x0, other arithmetic: 806 us -> none  [the longest x2 403 us: shards(): lax.all_gather(w_down[layer_idx], ('seq', 'batch'), axis=0, tiled=True)]
    all_gather x6 -> x4, waiting for transfers between devices: 626 us -> 83.4 us  [the longest x2 81.9 us: gather(): return lax.all_gather(a, BOTH, axis=0, tiled=True, axis_index_groups=ALL)]
    unnamed x11 -> x5, waiting for transfers between devices: 222 us -> 0.76 us
    psum x1 -> x0, waiting for transfers between devices: 212 us -> none  [shards(): lax.psum((stacked[0], stacked[1], stacked[2], stacked[3], stacked[4], sta...]
    reduce_scatter x2 -> x1, waiting for transfers between devices: 162 us -> 17.5 us  [shards(): lax.psum_scatter(parts, BOTH, scatter_dimension=0, axis_index_groups=SAME...]
    pallas_call x0 -> x13, Pallas kernels: none -> 144 us  [the longest x4 61.4 us: unpack(): pl.pallas_call(kernel, grid=(8,), out_shape=tuple((jax.ShapeDtypeStruct((...]
    reshape x13 -> x11, local copies, waits for them, and re-layouts: 132 us -> 4.14 us  [the longest x1 1.17 us: share(): w_up.reshape(-1, N_UP, 128)]
    dot_general x76, matrix products: 183 us -> 113 us  [the longest x28 54 us: dot_t(): lax.dot_general(a, b, (((1,), (1,)), ((), ())), preferred_element_type=F32)]
  transfers between devices with their start and end apart: 10 -> 51, of which waited for: 8 -> 22; matrix products, arithmetic and copies ran while one was open for 41% -> 27% of each run, Pallas kernels for 0% -> 19%
where the time goes in v1:
time: 625 us; the launch traced here: 615 us
  waiting for transfers between devices  176 us (28%)
  Pallas kernels  144 us (23%)
  matrix products  113 us (18%)
  starting transfers between devices  70.7 us (11%)
  local copies, waits for them, and re-layouts  41 us (7%)
  other arithmetic  33.6 us (5%)
  blocking collectives  18.9 us (3%)
  between operations  17.4 us (3%)
    all_gather x2, waiting for transfers between devices, gather(): return lax.all_gather(a, BOTH, axis=0, tiled=True, axis_index_groups=ALL)  81.9 us
    pallas_call x4, Pallas kernels, unpack(): pl.pallas_call(kernel, grid=(8,), out_shape=tuple((jax.ShapeDtypeStruct((...  61.4 us
    dot_general x28, matrix products, dot_t(): lax.dot_general(a, b, (((1,), (1,)), ((), ())), preferred_element_type=F32)  54 us
    dot_general x28, matrix products, dot(): return jnp.dot(a, b, preferred_element_type=F32)  46 us
    pallas_call x2, Pallas kernels, attend_fwd(): pl.pallas_call(fwd_kernel, grid=(PAIRS,), out_shape=(FLAT, FLAT), in_spec...  24.7 us
    pallas_call x2, Pallas kernels, attend_dkv(): pl.pallas_call(dkv_kernel, grid=(PAIRS,), out_shape=(part, part), in_spec...  23.3 us
    ppermute x14, waiting for transfers between devices, ring_start(): return (lax.ppermute(block, 'seq', UP), lax.ppermute(block, 'seq', DOWN))  22.5 us
    ppermute x14, starting transfers between devices, ring_start(): return (lax.ppermute(block, 'seq', UP), lax.ppermute(block, 'seq', DOWN))  21.6 us
  transfers between devices with their start and end apart: 51, of which 22 were waited for; matrix products, arithmetic and copies ran while one was open for 27% of the time, Pallas kernels for 19%

profile of v1, /device:TPU:1, one launch (start us, length us, event | category | flops | bytes accessed | tf_op | source)
XLA Modules:
  0.0 615.1 jit_solution(14067436331589210292)
XLA Ops:
  20.8 9.4 %psum.15 = s32[2,1024]{1,0:T(2,128)S(1)} all-reduce(s32[2,1024]{1,0:T(2,128)S(1)} %dynamic_update_slice.7), channel_id=1, replica_groups=mesh['seq'=16,'batch'=8] {'seq'}, use_global_device_ids=true, to_apply=%region_1.2 | all-reduce | flops 2048 | bytes 16384 | tf_op jit(solution)/shard_map/psum | solution.py:609
  40.0 9.6 %psum.14 = s32[16]{0:T(128)} all-reduce(s32[16]{0:T(128)S(1)} %dynamic_update_slice.6), channel_id=1, replica_groups=mesh['seq'=16,'batch'=8] {'batch'}, use_global_device_ids=true, to_apply=%region_0.1 | all-reduce | flops 16 | bytes 128 | tf_op jit(solution)/shard_map/psum | solution.py:624
  52.2 81.9 %all-gather.8.cloned.1.call-done = bf16[155648,128]{1,0:T(8,128)(2,1)} async-done(((bf16[1216,128]{1,0:T(8,128)(2,1)}), bf16[155648,128]{1,0:T(8,128)(2,1)}) %all-gather.8.cloned.1.call-update) | async-done | bytes 39845904 | tf_op jit(solution)/shard_map/all_gather | solution.py:588
  134.1 11.1 %shard_map.276 = (bf16[1088,1152]{1,0:T(8,128)(2,1)S(1)}, bf16[1088,2304]{1,0:T(8,128)(2,1)}, bf16[1088,1088]{1,0:T(8,128)(2,1)S(1)}) custom-call(bf16[2,2,4,4,2,1216,128]{6,5,4,3,2,1,0:T(8,128)(2,1)} %bitcast.352), custom_call_target="tpu_custom_call" | custom-call | bytes 20971520 | tf_op jit(solution)/shard_map/pallas_call | solution.py:552
  145.2 5.2 fusion.258
  156.5 19.3 %shard_map.277 = (bf16[1088,4352]{1,0:T(8,128)(2,1)}, bf16[4352,1088]{1,0:T(8,128)(2,1)}) custom-call(bf16[2,2,4,4,2,1216,128]{6,5,4,3,2,1,0:T(8,128)(2,1)} %bitcast.353, bf16[2,2,4,4,2,1216,128]{6,5,4,3,2,1,0:T(8,128)(2,1)} %bitcast.354), custom_call_target="tpu_custom_call" | custom-call | bytes 41943040 | tf_op jit(solution)/shard_map/pallas_call | solution.py:552
  182.0 11.5 %shard_map.278 = (bf16[1088,1152]{1,0:T(8,128)(2,1)S(1)}, bf16[1088,2304]{1,0:T(8,128)(2,1)}, bf16[1088,1088]{1,0:T(8,128)(2,1)S(1)}) custom-call(bf16[2,2,4,4,2,1216,128]{6,5,4,3,2,1,0:T(8,128)(2,1)} %bitcast.355), custom_call_target="tpu_custom_call" | custom-call | bytes 20971520 | tf_op jit(solution)/shard_map/pallas_call | solution.py:552
  201.9 12.5 %shard_map.279 = (bf16[128,1152]{1,0:T(8,128)(2,1)S(1)}, bf16[128,1152]{1,0:T(8,128)(2,1)S(1)}) custom-call(bf16[128,1152]{1,0:T(8,128)(2,1)S(1)} %copy-done.12, bf16[4,2,64,2304]{3,2,1,0:T(8,128)(2,1)S(1)} %pad_maximum_fusion.ko_ref.vo_ref, bf16[4,2,64,2304]{3,2,1,0:T(8,128)(2,1)} %collective-permute-done.5.ks_ref.vs_ref, ...), custom_call_target="tpu_custom_call" | custom-call | flops 1207959552 | bytes 6291456 | tf_op jit(solution)/shard_map/pallas_call | solution.py:318
  221.8 7.4 %multiply_convert_fusion.1 = (bf16[128,4352]{1,0:T(8,128)(2,1)S(1)}, f32[128,4352]{1,0:T(8,128)}) fusion(f32[128,4352]{1,0:T(8,128)S(1)} %fusion.128, bf16[128,1088]{0,1:T(8,128)(2,1)S(1)} %multiply_convert_fusion.4, bf16[1088,4352]{1,0:T(8,128)(2,1)S(1)} %bitcast.359), kind=kOutput, calls=%fused_computation.63 | convolution fusion | flops 1248919552 | bytes 15319040 | tf_op jit(solution)/shard_map/dot_general | solution.py:57
  246.6 19.5 %shard_map.280 = (bf16[1088,4352]{1,0:T(8,128)(2,1)}, bf16[4352,1088]{1,0:T(8,128)(2,1)}) custom-call(bf16[2,2,4,4,2,608,128]{6,5,4,3,2,1,0:T(8,128)(2,1)} %bitcast.356, bf16[2,2,4,4,2,608,128]{6,5,4,3,2,1,0:T(8,128)(2,1)} %bitcast.357), custom_call_target="tpu_custom_call" | custom-call | bytes 41943040 | tf_op jit(solution)/shard_map/pallas_call | solution.py:552
  290.6 12.3 %shard_map.281 = (bf16[128,1152]{1,0:T(8,128)(2,1)S(1)}, bf16[128,1152]{1,0:T(8,128)(2,1)S(1)}) custom-call(bf16[128,1152]{1,0:T(8,128)(2,1)S(1)} %copy-done.13, bf16[4,2,64,2304]{3,2,1,0:T(8,128)(2,1)} %pad_maximum_fusion.1.ko_ref.vo_ref, bf16[4,2,64,2304]{3,2,1,0:T(8,128)(2,1)} %collective-permute-done.14.ks_ref.vs_ref, ...), custom_call_target="tpu_custom_call" | custom-call | flops 1207959552 | bytes 6291456 | tf_op jit(solution)/shard_map/pallas_call | solution.py:318
  309.8 6.3 %multiply_convert_fusion = (bf16[128,4352]{1,0:T(8,128)(2,1)S(1)}, f32[128,4352]{1,0:T(8,128)S(1)}) fusion(f32[128,4352]{1,0:T(8,128)S(1)} %fusion.125, bf16[128,1088]{0,1:T(8,128)(2,1)S(1)} %multiply_convert_fusion.2, bf16[1088,4352]{1,0:T(8,128)(2,1)S(1)} %bitcast.363), kind=kOutput, calls=%fused_computation.50 | convolution fusion | flops 1248919552 | bytes 15319040 | tf_op jit(solution)/shard_map/dot_general | solution.py:57
  316.1 9.3 %add_convert_fusion.1 = bf16[128,4352]{1,0:T(8,128)(2,1)S(1)} fusion(f32[128,4352]{1,0:T(8,128)S(1)} %fusion.26, bf16[128,1088]{1,0:T(8,128)(2,1)S(1)} %bitcast.377, bf16[4352,1088]{1,0:T(8,128)(2,1)} %get-tuple-element.138, f32[128,4352]{1,0:T(8,128)S(1)} %get-tuple-element.259), kind=kOutput, calls=%fused_computation.49 | convolution fusion | flops 1252818944 | bytes 15319040 | tf_op jit(solution)/shard_map/dot_general | solution.py:61
  335.2 7.1 %convolution_add_fusion.16 = f32[128,1088]{0,1:T(8,128)S(1)} fusion(f32[128,1088]{0,1:T(8,128)S(1)} %fusion.60, bf16[128,4352]{1,0:T(8,128)(2,1)S(1)} %get-tuple-element.137, bf16[4352,1088]{1,0:T(8,128)(2,1)} %get-tuple-element.138), kind=kOutput, calls=%fused_computation.29 | convolution fusion | flops 1212293120 | bytes 11698176 | tf_op jit(solution)/shard_map/dot_general | solution.py:57
  351.9 10.5 %shard_map.282 = bf16[128,1152]{1,0:T(8,128)(2,1)S(1)} custom-call(bf16[128,1152]{1,0:T(8,128)(2,1)S(1)} %get-tuple-element.133.qe_ref.qx_ref, bf16[128,1152]{1,0:T(8,128)(2,1)S(1)} %pad_maximum_fusion.13.ge_ref.gx_ref, bf16[128,1152]{1,0:T(8,128)(2,1)S(1)} %get-tuple-element.133.qe_ref.qx_ref, bf16[128,1152]{1,0:T(8,128)(2,1)S(1)} %pad_maximum_fusion.13.ge_ref.gx_ref, ...), custom_call_target="tpu_custom_call" | custom-call | flops 2415919104 | bytes 6291456 | tf_op jit(solution)/shard_map/pallas_call | solution.py:335
  376.1 11.6 %shard_map.283 = (bf16[2,64,1152]{2,1,0:T(8,128)(2,1)S(1)}, bf16[2,64,1152]{2,1,0:T(8,128)(2,1)S(1)}) custom-call(bf16[2,64,2304]{2,1,0:T(8,128)(2,1)} %bitcast.38.k_ref.v_ref, bf16[2,64,2304]{2,1,0:T(8,128)(2,1)} %bitcast.38.k_ref.v_ref, bf16[4,2,64,1152]{3,2,1,0:T(8,128)(2,1)S(1)} %pad_maximum_fusion.5.qo_ref.qxo_ref, ...), custom_call_target="tpu_custom_call" | custom-call | flops 3623878656 | bytes 6291456 | tf_op jit(solution)/shard_map/pallas_call | solution.py:353
  402.4 9.4 %add_convert_fusion = bf16[128,4352]{1,0:T(8,128)(2,1)S(1)} fusion(f32[128,4352]{1,0:T(8,128)S(1)} %fusion.30, bf16[4352,1088]{1,0:T(8,128)(2,1)} %get-tuple-element.122, f32[128,4352]{1,0:T(8,128)} %get-tuple-element.254, f32[128,1088]{0,1:T(8,128)S(1)} %multiply_add_fusion.2), kind=kOutput, calls=%fused_computation.48 | convolution fusion | flops 1252958208 | bytes 15597568 | tf_op jit(solution)/shard_map/dot_general | solution.py:61
  432.1 17.5 %reduce-scatter.2.cloned.1.call-done = f32[1,16,2304]{2,1,0:T(8,128)} async-done(((f32[8,16,2304]{2,1,0:T(8,128)}), f32[1,16,2304]{2,1,0:T(8,128)}) %reduce-scatter.2.cloned.1.call-update) | async-done | bytes 147472 | tf_op jit(solution)/shard_map/reduce_scatter | solution.py:753
  449.7 10.4 %shard_map.284 = bf16[128,1152]{1,0:T(8,128)(2,1)S(1)} custom-call(bf16[128,1152]{1,0:T(8,128)(2,1)S(1)} %get-tuple-element.117.qe_ref.qx_ref, bf16[128,1152]{1,0:T(8,128)(2,1)S(1)} %pad_maximum_fusion.14.ge_ref.gx_ref, bf16[128,1152]{1,0:T(8,128)(2,1)S(1)} %get-tuple-element.117.qe_ref.qx_ref, bf16[128,1152]{1,0:T(8,128)(2,1)S(1)} %pad_maximum_fusion.14.ge_ref.gx_ref, ...), custom_call_target="tpu_custom_call" | custom-call | flops 2415919104 | bytes 6291456 | tf_op jit(solution)/shard_map/pallas_call | solution.py:335
  479.5 11.7 %shard_map.285 = (bf16[2,64,1152]{2,1,0:T(8,128)(2,1)S(1)}, bf16[2,64,1152]{2,1,0:T(8,128)(2,1)S(1)}) custom-call(bf16[2,64,2304]{2,1,0:T(8,128)(2,1)S(1)} %bitcast.349, bf16[2,64,2304]{2,1,0:T(8,128)(2,1)S(1)} %bitcast.350, bf16[4,2,64,1152]{3,2,1,0:T(8,128)(2,1)} %pad_maximum_fusion.4.qo_ref.qxo_ref, ...), custom_call_target="tpu_custom_call" | custom-call | flops 3623878656 | bytes 6291456 | tf_op jit(solution)/shard_map/pallas_call | solution.py:353
  498.0 9.3 %all-to-all-done = bf16[8,16,2304]{2,1,0:T(8,128)(2,1)S(1)} async-done(((bf16[8,16,2304]{2,1,0:T(8,128)(2,1)}), bf16[8,16,2304]{2,1,0:T(8,128)(2,1)S(1)}, u32[]{:S(2)}, u32[]{:S(2)}) %all-to-all-start) | async-done | bytes 589856 | tf_op jit(solution)/shard_map/all_to_all | solution.py:732
  542.3 22.4 %collective-permute-done.41 = bf16[2,1152,128]{2,1,0:T(8,128)(2,1)S(1)} collective-permute-done((bf16[2,1152,128]{2,1,0:T(8,128)(2,1)S(1)}, bf16[2,1152,128]{2,1,0:T(8,128)(2,1)S(1)}, u32[]{:S(2)}, u32[]{:S(2)}) %collective-permute-start.41) | collective-permute-done | bytes 589856 | tf_op jit(solution)/shard_map/ppermute | solution.py:371
  589.0 5.5 collective-permute-done.32
  597.0 11.1 %shard_map.288 = (f32[2,1088,128]{2,1,0:T(8,128)}, f32[2,1088,128]{2,1,0:T(8,128)}, f32[2,1088,128]{2,1,0:T(8,128)}, f32[2,4352,128]{2,1,0:T(8,128)}, f32[2,3264...) custom-call(s32[8]{0:T(128)} %fusion.199.place, ...), custom_call_target="tpu_custom_call" | custom-call | bytes 29360128 | tf_op jit(solution)/shard_map/pallas_call | solution.py:453
  (664 shorter events, 255.9 us)
Async XLA Ops:
  7.2 126.9 %all-gather.8.cloned.1.call-start = ((), (), s32[]{:S(2)}) async-start(), calls=%async_computation.2 | async-start | bytes 40157184 | tf_op jit(solution)/shard_map/all_gather | solution.py:588
  13.6 233.0 %all-gather.10.cloned.1.call-start = ((), (), s32[]{:S(2)}) async-start(), calls=%async_computation.4 | async-start | bytes 20078592 | tf_op jit(solution)/shard_map/all_gather | solution.py:588
  14.4 435.3 %reduce-scatter.2.cloned.1.call-start = ((), (), s32[]{:S(2)}) async-start(), calls=%async_computation.3 | async-start | bytes 1327104 | tf_op jit(solution)/shard_map/reduce_scatter | solution.py:753
  16.0 34.3 %collective-permute-start = (bf16[2,64,1088]{2,1,0:T(8,128)(2,1)}, bf16[2,64,1088]{2,1,0:T(8,128)(2,1)S(1)}, u32[]{:S(2)}, u32[]{:S(2)}) collective-permute-start(bf16[2,64,1088]{2,1,0:T(8,128)(2,1)} %pad_maximum_fusion.12), channel_id=1, source_target_pairs={{0,64},{8,72},{16,80},{24,88},{32,96},{40,104},{48,112},{56,120},{... | collective-permute-start | bytes 835592 | tf_op jit(solution)/shard_map/ppermute | solution.py:602
  150.8 26.6 %collective-permute-start.1 = (bf16[2,64,2304]{2,1,0:T(8,128)(2,1)S(1)}, bf16[2,64,2304]{2,1,0:T(8,128)(2,1)}, u32[]{:S(2)}, u32[]{:S(2)}) collective-permute-start(bf16[2,64,2304]{2,1,0:T(8,128)(2,1)S(1)} %bitcast.346), channel_id=1, source_target_pairs={{0,16},{8,24},{16,32},{24,40},{32,48},{40,56},{48,0},{56,8},{64,80... | collective-permute-start | bytes 1769480 | tf_op jit(solution)/shard_map/ppermute | solution.py:371
  152.1 25.4 %collective-permute-start.2 = (bf16[2,64,2304]{2,1,0:T(8,128)(2,1)S(1)}, bf16[2,64,2304]{2,1,0:T(8,128)(2,1)}, u32[]{:S(2)}, u32[]{:S(2)}) collective-permute-start(bf16[2,64,2304]{2,1,0:T(8,128)(2,1)S(1)} %bitcast.347), channel_id=1, source_target_pairs={{0,48},{8,56},{16,0},{24,8},{32,16},{40,24},{48,32},{56,40},{64,11... | collective-permute-start | bytes 1769480 | tf_op jit(solution)/shard_map/ppermute | solution.py:371
  178.5 15.0 %collective-permute-start.4 = (bf16[64,2304]{1,0:T(8,128)(2,1)S(1)}, bf16[64,2304]{1,0:T(8,128)(2,1)S(1)}, u32[]{:S(2)}, u32[]{:S(2)}) collective-permute-start(bf16[64,2304]{1,0:T(8,128)(2,1)S(1)} %slice_bitcast_fusion.4), channel_id=1, source_target_pairs={{0,48},{8,56},{16,0},{24,8},{32,16},{40,24},{48,32},{56,40},{64,11... | collective-permute-start | bytes 884744 | tf_op jit(solution)/shard_map/ppermute | solution.py:376
  214.4 14.9 %collective-permute-start.6 = (bf16[2,64,1152]{2,1,0:T(8,128)(2,1)S(1)}, bf16[2,64,1152]{2,1,0:T(8,128)(2,1)S(1)}, u32[]{:S(2)}, u32[]{:S(2)}) collective-permute-start(bf16[2,64,1152]{2,1,0:T(8,128)(2,1)S(1)} %bitcast.340), channel_id=1, source_target_pairs={{0,16},{8,24},{16,32},{24,40},{32,48},{40,56},{48,0},{56,8},{64,80... | collective-permute-start | bytes 884744 | tf_op jit(solution)/shard_map/ppermute | solution.py:371
  243.9 24.1 %collective-permute-start.10 = (bf16[2,64,2304]{2,1,0:T(8,128)(2,1)}, bf16[2,64,2304]{2,1,0:T(8,128)(2,1)}, u32[]{:S(2)}, u32[]{:S(2)}) collective-permute-start(bf16[2,64,2304]{2,1,0:T(8,128)(2,1)} %bitcast.38.k_ref.v_ref), channel_id=1, source_target_pairs={{0,16},{8,24},{16,32},{24,40},{32,48},{40,56},{48,0},{56,8},{64,80... | collective-permute-start | bytes 1769480 | tf_op jit(solution)/shard_map/ppermute | solution.py:371
  243.9 24.1 %collective-permute-start.11 = (bf16[2,64,2304]{2,1,0:T(8,128)(2,1)}, bf16[2,64,2304]{2,1,0:T(8,128)(2,1)}, u32[]{:S(2)}, u32[]{:S(2)}) collective-permute-start(bf16[2,64,2304]{2,1,0:T(8,128)(2,1)} %bitcast.38.k_ref.v_ref), channel_id=1, source_target_pairs={{0,48},{8,56},{16,0},{24,8},{32,16},{40,24},{48,32},{56,40},{64,11... | collective-permute-start | bytes 1769480 | tf_op jit(solution)/shard_map/ppermute | solution.py:371
  302.9 27.9 %collective-permute-start.15 = (bf16[2,64,1152]{2,1,0:T(8,128)(2,1)S(1)}, bf16[2,64,1152]{2,1,0:T(8,128)(2,1)S(1)}, u32[]{:S(2)}, u32[]{:S(2)}) collective-permute-start(bf16[2,64,1152]{2,1,0:T(8,128)(2,1)S(1)} %bitcast.343), channel_id=1, source_target_pairs={{0,16},{8,24},{16,32},{24,40},{32,48},{40,56},{48,0},{56,8},{64,80... | collective-permute-start | bytes 884744 | tf_op jit(solution)/shard_map/ppermute | solution.py:371
  302.9 27.8 %collective-permute-start.16 = (bf16[2,64,1152]{2,1,0:T(8,128)(2,1)S(1)}, bf16[2,64,1152]{2,1,0:T(8,128)(2,1)S(1)}, u32[]{:S(2)}, u32[]{:S(2)}) collective-permute-start(bf16[2,64,1152]{2,1,0:T(8,128)(2,1)S(1)} %bitcast.344), channel_id=1, source_target_pairs={{0,48},{8,56},{16,0},{24,8},{32,16},{40,24},{48,32},{56,40},{64,11... | collective-permute-start | bytes 884744 | tf_op jit(solution)/shard_map/ppermute | solution.py:371
  346.7 16.6 %collective-permute-start.20 = (bf16[2,64,1152]{2,1,0:T(8,128)(2,1)S(1)}, bf16[2,64,1152]{2,1,0:T(8,128)(2,1)S(1)}, u32[]{:S(2)}, u32[]{:S(2)}) collective-permute-start(bf16[2,64,1152]{2,1,0:T(8,128)(2,1)S(1)} %bitcast.337), channel_id=1, source_target_pairs={{0,16},{8,24},{16,32},{24,40},{32,48},{40,56},{48,0},{56,8},{64,80... | collective-permute-start | bytes 884744 | tf_op jit(solution)/shard_map/ppermute | solution.py:371
  346.8 16.5 %collective-permute-start.21 = (bf16[2,64,1152]{2,1,0:T(8,128)(2,1)S(1)}, bf16[2,64,1152]{2,1,0:T(8,128)(2,1)S(1)}, u32[]{:S(2)}, u32[]{:S(2)}) collective-permute-start(bf16[2,64,1152]{2,1,0:T(8,128)(2,1)S(1)} %bitcast.338), channel_id=1, source_target_pairs={{0,48},{8,56},{16,0},{24,8},{32,16},{40,24},{48,32},{56,40},{64,11... | collective-permute-start | bytes 884744 | tf_op jit(solution)/shard_map/ppermute | solution.py:371
  350.2 24.5 %collective-permute-start.24 = (bf16[4,2,64,1152]{3,2,1,0:T(8,128)(2,1)S(1)}, bf16[4,2,64,1152]{3,2,1,0:T(8,128)(2,1)S(1)}, u32[]{:S(2)}, u32[]{:S(2)}) collective-permute-start(bf16[4,2,64,1152]{3,2,1,0:T(8,128)(2,1)S(1)} %pad_maximum_fusion.5.qo_ref.qxo_ref), channel_id=1, source_target_pairs={{0,8},{8,0},{16,24},{24,16},{32,40},{40,32},{48,56},{56,48},{64,72... | collective-permute-start | bytes 3538952 | tf_op jit(solution)/shard_map/ppermute | solution.py:381
  373.6 104.3 %collective-permute-start.30 = (bf16[4,2,64,1152]{3,2,1,0:T(8,128)(2,1)}, bf16[4,2,64,1152]{3,2,1,0:T(8,128)(2,1)}, u32[]{:S(2)}, u32[]{:S(2)}) collective-permute-start(bf16[4,2,64,1152]{3,2,1,0:T(8,128)(2,1)} %pad_maximum_fusion.4.qo_ref.qxo_ref), channel_id=1, source_target_pairs={{0,8},{8,0},{16,24},{24,16},{32,40},{40,32},{48,56},{56,48},{64,72... | collective-permute-start | bytes 3538952 | tf_op jit(solution)/shard_map/ppermute | solution.py:381
  420.4 98.5 %all-gather.12.cloned.1.call-start = ((), (), s32[]{:S(2)}) async-start(), calls=%async_computation.5 | async-start | bytes 1253376 | tf_op jit(solution)/shard_map/all_gather | solution.py:716
  424.5 35.6 %collective-permute-start.26 = (bf16[2,64,1152]{2,1,0:T(8,128)(2,1)S(1)}, bf16[2,64,1152]{2,1,0:T(8,128)(2,1)}, u32[]{:S(2)}, u32[]{:S(2)}) collective-permute-start(bf16[2,64,1152]{2,1,0:T(8,128)(2,1)S(1)} %bitcast.334), channel_id=1, source_target_pairs={{0,16},{8,24},{16,32},{24,40},{32,48},{40,56},{48,0},{56,8},{64,80... | collective-permute-start | bytes 884744 | tf_op jit(solution)/shard_map/ppermute | solution.py:371
  424.8 35.3 %collective-permute-start.27 = (bf16[2,64,1152]{2,1,0:T(8,128)(2,1)S(1)}, bf16[2,64,1152]{2,1,0:T(8,128)(2,1)}, u32[]{:S(2)}, u32[]{:S(2)}) collective-permute-start(bf16[2,64,1152]{2,1,0:T(8,128)(2,1)S(1)} %bitcast.335), channel_id=1, source_target_pairs={{0,48},{8,56},{16,0},{24,8},{32,16},{40,24},{48,32},{56,40},{64,11... | collective-permute-start | bytes 884744 | tf_op jit(solution)/shard_map/ppermute | solution.py:371
  497.1 99.9 %all-gather.14.cloned.1.call-start = ((), (), s32[]{:S(2)}) async-start(), calls=%async_computation.6 | async-start | bytes 5308416 | tf_op jit(solution)/shard_map/all_gather | solution.py:737
  535.6 29.1 %collective-permute-start.41 = (bf16[2,1152,128]{2,1,0:T(8,128)(2,1)S(1)}, bf16[2,1152,128]{2,1,0:T(8,128)(2,1)S(1)}, u32[]{:S(2)}, u32[]{:S(2)}) collective-permute-start(bf16[2,1152,128]{2,1,0:T(8,128)(2,1)S(1)} %bitcast.330), channel_id=1, source_target_pairs={{0,48},{8,56},{16,0},{24,8},{32,16},{40,24},{48,32},{56,40},{64,11... | collective-permute-start | bytes 1769480 | tf_op jit(solution)/shard_map/ppermute | solution.py:371
  541.4 27.0 %collective-permute-start.40 = (bf16[2,1152,128]{2,1,0:T(8,128)(2,1)S(1)}, bf16[2,1152,128]{2,1,0:T(8,128)(2,1)S(1)}, u32[]{:S(2)}, u32[]{:S(2)}) collective-permute-start(bf16[2,1152,128]{2,1,0:T(8,128)(2,1)S(1)} %bitcast.331), channel_id=1, source_target_pairs={{0,16},{8,24},{16,32},{24,40},{32,48},{40,56},{48,0},{56,8},{64,80... | collective-permute-start | bytes 1769480 | tf_op jit(solution)/shard_map/ppermute | solution.py:371
  541.7 45.4 %collective-permute-start.19 = (bf16[64,1088]{1,0:T(8,128)(2,1)S(1)}, bf16[64,1088]{1,0:T(8,128)(2,1)}, u32[]{:S(2)}, u32[]{:S(2)}) collective-permute-start(bf16[64,1088]{1,0:T(8,128)(2,1)S(1)} %get-tuple-element.234), channel_id=1, source_target_pairs={{0,64},{8,72},{16,80},{24,88},{32,96},{40,104},{48,112},{56,120},{... | collective-permute-start | bytes 417800 | tf_op jit(solution)/shard_map/ppermute | solution.py:759
  578.0 19.0 %collective-permute-start.44 = (bf16[4,2,1152,128]{3,2,1,0:T(8,128)(2,1)}, bf16[4,2,1152,128]{3,2,1,0:T(8,128)(2,1)}, u32[]{:S(2)}, u32[]{:S(2)}) collective-permute-start(bf16[4,2,1152,128]{3,2,1,0:T(8,128)(2,1)} %pad_maximum_fusion.3), channel_id=1, source_target_pairs={{0,8},{8,0},{16,24},{24,16},{32,40},{40,32},{48,56},{56,48},{64,72... | collective-permute-start | bytes 7077896 | tf_op jit(solution)/shard_map/ppermute | solution.py:381
  (183 other events, 2199.0 us)
Sparse Core Ops, SparseCore 0:
  13.8 120.2 all-gather.7
  137.1 85.8 all-gather.9
  420.5 29.1 reduce-scatter.1
  478.0 40.8 all-gather.11
  522.2 48.2 all-gather.13
